TPU v7x, 32 devices: a whole 2x2x4 slice. The times are simulated.
32 devices in a mesh: groups: 2 (over y), blk: 4 (over x, core), fetch: 4 (over z).
Axes of the slice: x: 2, y: 2, z: 4, core: 2. Of those that a mesh axis runs over, the one named last changes fastest.
Arguments:
- amplitudes: bfloat16 [3584, 3072], P(('groups', 'fetch'), 'blk'), parts along dimension 0, may hold values from -6 to 6
- integrals: bfloat16 [8, 12, 256, 1024], P(('groups', 'blk'), 'fetch'), parts along dimension 0, may hold values from -0.15625 to 0.15625
- tile_ids: int32 [8, 12], P(('groups', 'blk')), parts along dimension 0, may hold values from -1 to 11, as said below
Outputs:
- ladder: bfloat16 [3584, 4096], P(('groups', 'fetch'), 'blk'), parts along dimension 0
There are 2 independent parts, one for each index of `groups`. A program takes and returns all parts, laid end to end along the dimension named above; each array names one. Nothing has to cross between parts.
Inputs may be any that keep to these rules, and one draw needn't show every extreme that they name: `tile_ids`: row r gives 4 owners in turn, 3 slots each: an owner's tiles first, then -1 in its empty slots. Every owner holds at least one tile, in every row some owner holds 3, and the tiles named in one row are distinct.
All inputs are finite; a program needn't handle non-finite values.
Results may differ from a plain program's by a relative error of at most 0.001.
Values may be sent and summed in bfloat16 or wider, within the bound.
A program may use at most 128 MiB of HBM per device.

v0:
```python
import jax
import jax.numpy as jnp
from jax import lax
from jax.sharding import PartitionSpec as P


def from_behind(value, axis, steps):
    count = lax.axis_size(axis)
    pairs = [(source, (source + steps) % count) for source in range(count)]
    return lax.ppermute(value, axis, pairs)


def per_device(amplitudes, integrals, tile_ids):
    gathered = lax.all_gather(integrals, "fetch", axis=1, tiled=True)
    stacked = gathered[0]
    owners = tile_ids[0]
    tile_width = stacked.shape[1]
    columns = stacked.shape[2]
    group_width = amplitudes.shape[1]
    cycle_size = lax.axis_size("blk")
    tile_count = group_width * cycle_size // tile_width
    wanted = jnp.arange(tile_count, dtype=jnp.int32)
    selector = (owners[None, :] == wanted[:, None]).astype(jnp.bfloat16)
    dense = jnp.einsum("ks,stc->ktc", selector, stacked, preferred_element_type=jnp.float32)
    dense = dense.astype(jnp.bfloat16).reshape(tile_count * tile_width, columns)

    def contract(running, piece, start):
        matching = lax.dynamic_slice_in_dim(dense, start, piece.shape[1], 0)
        return running + jnp.dot(piece, matching, preferred_element_type=jnp.float32)

    initial = jnp.zeros((amplitudes.shape[0], columns), jnp.float32)
    here = lax.axis_index("blk")

    def forward(current):
        return from_behind(current, "blk", 1)

    def advance_both(position, carry):
        accumulated, ahead, behind = carry
        ahead = forward(ahead)
        behind = from_behind(behind, "blk", -1)
        accumulated = contract(accumulated, ahead, (here - position) % cycle_size * group_width)
        accumulated = contract(accumulated, behind, (here + position) % cycle_size * group_width)
        return (accumulated, ahead, behind)

    running = contract(initial, amplitudes, here * group_width)
    running, ahead, behind = lax.fori_loop(
        1, (cycle_size + 1) // 2, advance_both, (running, amplitudes, amplitudes)
    )
    ahead = forward(ahead)
    running = contract(running, ahead, (here - cycle_size // 2) % cycle_size * group_width)
    return running.astype(jnp.bfloat16)


def solution(mesh):
    placed = (
        P(("groups", "fetch"), "blk"),
        P(("groups", "blk"), "fetch", None, None),
        P(("groups", "blk"), None),
    )
    return jax.shard_map(
        per_device,
        mesh=mesh,
        in_specs=placed,
        out_specs=P(("groups", "fetch"), "blk"),
        check_vma=False,
    )
```

profile of v0, /device:TPU:0, one launch (start us, length us, event | category | flops | bytes accessed | tf_op | source)
XLA Modules:
  0.0 155.4 jit_solution(14862046702412451543)
XLA Ops:
  6.5 0.0 all-gather.2.cloned.1.call-start
  6.5 0.7 all-gather.2.cloned.1.call-update
  7.3 0.5 collective-permute-start
  7.8 2.0 %collective-permute-start.1 = (bf16[448,768]{1,0:T(8,128)(2,1)}, bf16[448,768]{1,0:T(8,128)(2,1)S(1)}, u32[]{:S(2)}, u32[]{:S(2)}) collective-permute-start(bf16[448,768]{1,0:T(8,128)(2,1)} %param.3), channel_id=1, source_target_pairs={{0,12},{4,0},{8,4},{12,8},{1,13},{5,1},{9,5},{13,9},{2,14},{6,2},{... | collective-permute-start | bytes 2064392 | tf_op jit(solution)/shard_map/while/body/eval_jaxpr/ppermute | solution.py:10
  9.8 13.5 %collective-permute-done = bf16[448,768]{1,0:T(8,128)(2,1)S(1)} collective-permute-done((bf16[448,768]{1,0:T(8,128)(2,1)}, bf16[448,768]{1,0:T(8,128)(2,1)S(1)}, u32[]{:S(2)}, u32[]{:S(2)}) %collective-permute-start) | collective-permute-done | bytes 688160 | tf_op jit(solution)/shard_map/while/body/eval_jaxpr/ppermute | solution.py:10
  23.2 2.6 %collective-permute-start.2 = (bf16[448,768]{1,0:T(8,128)(2,1)S(1)}, bf16[448,768]{1,0:T(8,128)(2,1)S(1)}, u32[]{:S(2)}, u32[]{:S(2)}) collective-permute-start(bf16[448,768]{1,0:T(8,128)(2,1)S(1)} %collective-permute-done), channel_id=1, source_target_pairs={{0,4},{4,8},{8,12},{12,0},{1,5},{5,9},{9,13},{13,1},{2,6},{6,10},{... | collective-permute-start | bytes 2064392 | tf_op jit(solution)/shard_map/ppermute | solution.py:10
  25.9 101.2 %all-gather.2.cloned.1.call-done = bf16[1,12,256,1024]{3,2,0,1:T(8,128)(2,1)} async-done(((bf16[1,3,256,1024]{3,2,0,1:T(8,128)(2,1)}), bf16[1,12,256,1024]{3,2,0,1:T(8,128)(2,1)}) %all-gather.2.cloned.1.call-update) | async-done | bytes 6291472 | tf_op jit(solution)/shard_map/all_gather | solution.py:14
  127.0 7.8 %fusion.3 = bf16[12,256,1024]{2,0,1:T(8,128)(2,1)S(1)} fusion(bf16[1,12,256,1024]{3,2,0,1:T(8,128)(2,1)} %all-gather.2.cloned.1.call-done, s32[12]{0:T(128)} %bitcast.22), kind=kOutput, calls=%fused_computation.3 | convolution fusion | flops 78643344 | bytes 12582960 | tf_op jit(solution)/shard_map/ks,stc->ktc/dot_general | solution.py:24
  134.8 0.0 copy-start.1
  134.8 6.2 %copy.9 = bf16[12,256,1024]{2,1,0:T(8,128)(2,1)} copy(bf16[12,256,1024]{2,0,1:T(8,128)(2,1)S(1)} %fusion.3) | data formatting | bytes 12582912 | tf_op jit(solution)/shard_map/convert_element_type | solution.py:25
  141.0 0.0 copy-done.1
  141.0 0.0 copy-start
  141.0 2.4 %fusion.12 = f32[1024,448]{0,1:T(8,128)S(1)} fusion(bf16[448,768]{1,0:T(8,128)(2,1)S(1)} %copy-done.1, bf16[3072,1024]{1,0:T(8,128)(2,1)} %bitcast.17, s32[]{:T(128)S(6)} %select_n.32), kind=kOutput, calls=%fused_computation.11 | convolution fusion | flops 704643072 | bytes 4096004 | tf_op jit(solution)/shard_map/dot_general | solution.py:29
  143.4 2.3 %fusion.10 = f32[1024,448]{0,1:T(8,128)S(1)} fusion(bf16[448,768]{1,0:T(8,128)(2,1)S(1)} %collective-permute-done, bf16[3072,1024]{1,0:T(8,128)(2,1)} %bitcast.18, s32[]{:T(128)S(6)} %select_n.34), kind=kOutput, calls=%fused_computation.9 | convolution fusion | flops 704643072 | bytes 4096004 | tf_op jit(solution)/shard_map/while/body/eval_jaxpr/dot_general | solution.py:29
  145.7 0.0 collective-permute-done.1
  145.7 0.0 copy-done
  145.7 0.9 fusion.8
  146.6 0.0 collective-permute-done.2
  146.7 1.9 %fusion.16 = bf16[448,1024]{1,0:T(8,128)(2,1)} fusion(bf16[448,768]{1,0:T(8,128)(2,1)S(1)} %collective-permute-done.2, bf16[3072,1024]{1,0:T(8,128)(2,1)S(1)} %bitcast.20, s32[]{:T(128)S(6)} %select_n.38, f32[1024,448]{0,1:T(8,128)S(1)} %fusion.8, f32[1024,448]{0,1:T(8,128)S(1)} %fusion.12, f32[1024,448]{0,1:T(8,128)S(1)} %fusion.10), kind=kOutput, calls=%fused_computation.13 | convolution fusion | flops 706478080 | bytes 8683524 | tf_op jit(solution)/shard_map/dot_general | solution.py:29
Async XLA Ops:
  6.5 120.5 %all-gather.2.cloned.1.call-start = ((), (), s32[]{:S(2)}) async-start(), calls=%async_computation | async-start | bytes 7864320 | tf_op jit(solution)/shard_map/all_gather | solution.py:14
  7.3 16.0 %collective-permute-start = (bf16[448,768]{1,0:T(8,128)(2,1)}, bf16[448,768]{1,0:T(8,128)(2,1)S(1)}, u32[]{:S(2)}, u32[]{:S(2)}) collective-permute-start(bf16[448,768]{1,0:T(8,128)(2,1)} %param.3), channel_id=1, source_target_pairs={{0,4},{4,8},{8,12},{12,0},{1,5},{5,9},{9,13},{13,1},{2,6},{6,10},{... | collective-permute-start | bytes 2064392 | tf_op jit(solution)/shard_map/while/body/eval_jaxpr/ppermute | solution.py:10
  7.8 138.0 %collective-permute-start.1 = (bf16[448,768]{1,0:T(8,128)(2,1)}, bf16[448,768]{1,0:T(8,128)(2,1)S(1)}, u32[]{:S(2)}, u32[]{:S(2)}) collective-permute-start(bf16[448,768]{1,0:T(8,128)(2,1)} %param.3), channel_id=1, source_target_pairs={{0,12},{4,0},{8,4},{12,8},{1,13},{5,1},{9,5},{13,9},{2,14},{6,2},{... | collective-permute-start | bytes 2064392 | tf_op jit(solution)/shard_map/while/body/eval_jaxpr/ppermute | solution.py:10
  23.2 123.4 %collective-permute-start.2 = (bf16[448,768]{1,0:T(8,128)(2,1)S(1)}, bf16[448,768]{1,0:T(8,128)(2,1)S(1)}, u32[]{:S(2)}, u32[]{:S(2)}) collective-permute-start(bf16[448,768]{1,0:T(8,128)(2,1)S(1)} %collective-permute-done), channel_id=1, source_target_pairs={{0,4},{4,8},{8,12},{12,0},{1,5},{5,9},{9,13},{13,1},{2,6},{6,10},{... | collective-permute-start | bytes 2064392 | tf_op jit(solution)/shard_map/ppermute | solution.py:10
  134.8 6.2 %copy-start.1 = (bf16[448,768]{1,0:T(8,128)(2,1)S(1)}, bf16[448,768]{1,0:T(8,128)(2,1)}, u32[]{:S(2)}) copy-start(bf16[448,768]{1,0:T(8,128)(2,1)} %param.3) | copy-start | bytes 2064388
  141.0 4.7 %copy-start = (bf16[12,256,1024]{2,1,0:T(8,128)(2,1)S(1)}, bf16[12,256,1024]{2,1,0:T(8,128)(2,1)}, u32[]{:S(2)}) copy-start(bf16[12,256,1024]{2,1,0:T(8,128)(2,1)} %copy.9) | copy-start | bytes 18874372
Sparse Core Ops, SparseCore 0:
  8.9 118.0 all-gather.1
where the time goes:
time: 156 us; the launch traced here: 155 us
  waiting for transfers between devices  115 us (74%)
  matrix products  15.3 us (10%)
  between operations  13.4 us (9%)
  local copies, waits for them, and re-layouts  6.18 us (4%)
  starting transfers between devices  5.11 us (3%)
    all_gather x1, waiting for transfers between devices, per_device(): gathered = lax.all_gather(integrals, 'fetch', axis=1, tiled=True)  101 us
    ppermute x3, waiting for transfers between devices, from_behind(): return lax.ppermute(value, axis, pairs)  13.5 us
    dot_general x1, matrix products, per_device(): jnp.einsum('ks,stc->ktc', selector, stacked, preferred_element_type=jnp.f...  7.78 us
    dot_general x4, matrix products, contract(): jnp.dot(piece, matching, preferred_element_type=jnp.float32)  7.51 us
    convert_element_type x1, local copies, waits for them, and re-layouts, per_device(): dense = dense.astype(jnp.bfloat16).reshape(tile_count * tile_width, columns)  6.17 us
    ppermute x3, starting transfers between devices, from_behind(): return lax.ppermute(value, axis, pairs)  5.11 us
  transfers between devices with their start and end apart: 4, of which 2 were waited for; matrix products, arithmetic and copies ran while one was open for 13% of the time, Pallas kernels for 0%

commit v1 on v0

v1 whole, which is shorter than its diff:
```python
import functools

import jax
import jax.numpy as jnp
from jax import lax
from jax.experimental import pallas as pl
from jax.experimental.pallas import tpu as pltpu
from jax.sharding import PartitionSpec as P

CORES = 2
CHUNKS = 4
MESH = pl.DeviceIdType.MESH


def kernel(
    n, chips, lead,
    ids_ref, a_ref, b_ref, out_ref,
    abuf, aout, bbuf, acc, acc2, obuf, rbuf,
    local_sem, a_send, a_recv, s_send, s_recv, o_send, o_recv,
    p_send, m_send, b_recv, r_sem,
):
    g = lax.axis_index("groups")
    b = lax.axis_index("blk")
    f = lax.axis_index("fetch")
    x, core = lax.div(b, CORES), lax.rem(b, CORES)
    sibling = b + 1 - 2 * core
    slots, tile, columns = b_ref.shape[1:]
    step_rows = tile // CHUNKS
    per_group = a_ref.shape[1] // tile

    low = f < n // 2
    way = jnp.where(low, 1, -1)
    far_hops = jnp.where(low, n - 1 - f, f)
    near_hops = n - 1 - far_hops
    is_end = near_hops == 0
    is_helper = near_hops == 1
    far_side = (g, b, jnp.clip(f + way, 0, n - 1))
    near_side = (g, b, jnp.clip(f - way, 0, n - 1))
    has_near = near_hops > 0

    def mate(hop):
        return lax.rem(x + hop, chips) * CORES + core

    barrier = pltpu.get_barrier_semaphore()
    for hop in range(1, chips):
        pl.semaphore_signal(barrier, inc=1, device_id=(g, mate(hop), f), device_id_type=MESH)
    pl.semaphore_signal(barrier, inc=1, device_id=(g, sibling, f), device_id_type=MESH)
    pl.semaphore_signal(barrier, inc=1, device_id=far_side, device_id_type=MESH)

    @pl.when(has_near)
    def _():
        pl.semaphore_signal(barrier, inc=1, device_id=near_side, device_id_type=MESH)

    own_a = [
        pltpu.make_async_copy(
            a_ref.at[:, pl.ds(k * tile, tile)], abuf.at[b * per_group + k], local_sem.at[1 + k]
        )
        for k in range(per_group)
    ]
    own_b = pltpu.make_async_copy(b_ref.at[0], bbuf.at[f], local_sem.at[0])
    for copy in own_a:
        copy.start()
    own_b.start()
    pl.semaphore_wait(barrier, chips + 1 + jnp.where(has_near, 1, 0))

    def remote(src, dst, send, recv, device):
        return pltpu.make_async_remote_copy(
            src_ref=src, dst_ref=dst, send_sem=send, recv_sem=recv,
            device_id=device, device_id_type=MESH,
        )

    def b_copy(owner, slot, chunk, device, send, width, src=None):
        rows = pl.ds(chunk * step_rows, step_rows)
        piece = bbuf.at[owner, slot, rows, pl.ds(0, width)]
        source = piece if src is None else src.at[0, slot, rows, pl.ds(0, width)]
        return remote(source, piece, send.at[owner, slot, chunk], b_recv.at[owner, slot, chunk], device)

    def to_far(owner, slot, chunk, src=None):
        return b_copy(owner, slot, chunk, far_side, p_send, columns, src)

    def near_each(owner, slot, src, action):
        @pl.when(is_helper)
        def _():
            for chunk in range(CHUNKS):
                action(b_copy(owner, slot, chunk, near_side, m_send, lead, src))

        @pl.when(near_hops > 1)
        def _():
            for chunk in range(CHUNKS):
                action(b_copy(owner, slot, chunk, near_side, m_send, columns, src))

    def a_group(buffer, owner):
        return buffer.at[pl.ds(owner * per_group, per_group)]

    def a_mate(buffer, hop, base):
        part = a_group(buffer, b)
        return remote(part, part, a_send.at[base, hop], a_recv.at[base, hop], (g, mate(hop), f))

    def a_sib(buffer, hop, base):
        part = a_group(buffer, lax.rem(x + chips - hop, chips) * CORES + core)
        return remote(part, part, s_send.at[base, hop], s_recv.at[base, hop], (g, sibling, f))

    for copy in own_a:
        copy.wait()
    for hop in range(1, chips):
        a_mate(abuf, hop, 0).start()
    a_sib(abuf, 0, 0).start()

    a_help = remote(a_group(abuf, b), a_group(aout, b), o_send.at[0], o_recv.at[0], far_side)

    @pl.when(is_end)
    def _():
        a_help.start()

    for slot in range(slots):
        for chunk in range(CHUNKS):
            to_far(f, slot, chunk, b_ref).start()
        near_each(f, slot, b_ref, lambda copy: copy.start())

        if slot == 0:
            @pl.when(is_end)
            def _():
                a_help.wait_send()

    own_b.wait()
    for hop in range(1, chips):
        a_mate(abuf, hop, 0).wait_recv()
        a_sib(abuf, hop, 0).start()
    for hop in range(chips):
        a_sib(abuf, hop, 0).wait_recv()

    def a_tile(buffer, owner, slot):
        name = ids_ref[0, owner * slots + slot]
        empty = lax.shift_right_arithmetic(name, 31)
        value = buffer[name - empty]
        return value * (1 + empty).astype(jnp.float32).astype(value.dtype)

    def add(owner, slot):
        piece = a_tile(abuf, owner, slot)
        acc[:, :lead] += jnp.dot(piece, bbuf[owner, slot, :, :lead], preferred_element_type=jnp.float32)

        @pl.when(jnp.logical_not(is_end))
        def _():
            acc[:, lead:] += jnp.dot(piece, bbuf[owner, slot, :, lead:], preferred_element_type=jnp.float32)

    def add_help(owner, slot):
        piece = a_tile(aout, owner, slot)
        acc2[...] += jnp.dot(piece, bbuf[owner, slot, :, lead:], preferred_element_type=jnp.float32)

    acc[...] = jnp.zeros_like(acc)
    acc2[...] = jnp.zeros_like(acc2)

    def own_slot(slot, carry):
        add(f, slot)
        return carry

    lax.fori_loop(0, slots, own_slot, 0)

    last_owner = f + way * far_hops

    def step(j, carry):
        @pl.when(is_helper & (j == 2))
        def _():
            a_help.wait_recv()
            for hop in range(1, chips):
                a_mate(aout, hop, 1).start()
            a_sib(aout, 0, 1).start()

        @pl.when(is_helper & (j == 4))
        def _():
            for hop in range(1, chips):
                a_mate(aout, hop, 1).wait_recv()
                a_sib(aout, hop, 1).start()

        final = j == slots * far_hops - 1

        @pl.when(is_helper & final)
        def _():
            for hop in range(chips):
                a_sib(aout, hop, 1).wait_recv()

            def one(index, carry):
                owner, slot = lax.div(index, slots), lax.rem(index, slots)

                @pl.when(jnp.logical_not((owner == last_owner) & (slot == slots - 1)))
                def _():
                    add_help(owner, slot)
                return carry

            lax.fori_loop(0, n * slots, one, 0)

        @pl.when(j < slots * far_hops)
        def _():
            owner = f + way * (1 + lax.div(j, slots))
            slot = lax.rem(j, slots)

            @pl.when(is_end)
            def _():
                for chunk in range(CHUNKS):
                    b_copy(owner, slot, chunk, far_side, m_send, lead).wait_recv()

            @pl.when(is_helper)
            def _():
                for chunk in range(CHUNKS):
                    b_copy(owner, slot, chunk, far_side, m_send, columns).wait_recv()
                    b_copy(owner, slot, chunk, near_side, m_send, lead).start()

            @pl.when(near_hops > 1)
            def _():
                for chunk in range(CHUNKS):
                    b_copy(owner, slot, chunk, far_side, m_send, columns).wait_recv()
                    b_copy(owner, slot, chunk, near_side, m_send, columns).start()

            @pl.when(is_helper & final)
            def _():
                add_help(owner, slot)
                obuf[...] = acc2[...].astype(obuf.dtype)
                remote(obuf, rbuf, r_sem.at[0], r_sem.at[1], near_side).start()

            add(owner, slot)

        back = j - 1

        @pl.when((back >= 0) & (back < slots * near_hops))
        def _():
            owner = f - way * (1 + lax.div(back, slots))
            slot = lax.rem(back, slots)
            for chunk in range(CHUNKS):
                to_far(owner, slot, chunk).wait_recv()
                to_far(owner, slot, chunk).start()
            add(owner, slot)

        return carry

    lax.fori_loop(0, slots * (n - 1), step, 0)

    out_ref[:, :lead] = acc[:, :lead].astype(out_ref.dtype)
    result = remote(obuf, rbuf, r_sem.at[0], r_sem.at[1], near_side)

    @pl.when(is_end)
    def _():
        result.wait_recv()
        out_ref[:, lead:] = rbuf[...]

    @pl.when(jnp.logical_not(is_end))
    def _():
        out_ref[:, lead:] = acc[:, lead:].astype(out_ref.dtype)

    def far_done(k, carry):
        owner, slot = f - way * lax.div(k, slots), lax.rem(k, slots)
        for chunk in range(CHUNKS):
            to_far(owner, slot, chunk).wait_send()
        return carry

    lax.fori_loop(0, slots * (near_hops + 1), far_done, 0)

    @pl.when(has_near)
    def _():
        def near_done(k, carry):
            owner, slot = f + way * lax.div(k, slots), lax.rem(k, slots)
            near_each(owner, slot, None, lambda copy: copy.wait_send())
            return carry

        lax.fori_loop(0, slots * (far_hops + 1), near_done, 0)

    for hop in range(1, chips):
        a_mate(abuf, hop, 0).wait_send()
    for hop in range(chips):
        a_sib(abuf, hop, 0).wait_send()

    @pl.when(is_helper)
    def _():
        for hop in range(1, chips):
            a_mate(aout, hop, 1).wait_send()
        for hop in range(chips):
            a_sib(aout, hop, 1).wait_send()
        result.wait_send()


def per_device(mesh_shape, amplitudes, integrals, tile_ids):
    n, chips = mesh_shape["fetch"], mesh_shape["blk"] // CORES
    rows, width = amplitudes.shape
    _, slots, tile, columns = integrals.shape
    lead = columns * 5 // 8
    tiles = chips * CORES * width // tile
    bf16, f32, dma = jnp.bfloat16, jnp.float32, pltpu.SemaphoreType.DMA
    return pl.pallas_call(
        functools.partial(kernel, n, chips, lead),
        out_shape=jax.ShapeDtypeStruct((rows, columns), bf16),
        in_specs=[
            pl.BlockSpec(memory_space=pltpu.SMEM),
            pl.BlockSpec(memory_space=pl.ANY),
            pl.BlockSpec(memory_space=pl.ANY),
        ],
        out_specs=pl.BlockSpec(memory_space=pltpu.VMEM),
        scratch_shapes=[
            pltpu.VMEM((tiles, rows, tile), bf16),
            pltpu.VMEM((tiles, rows, tile), bf16),
            pltpu.VMEM((n, slots, tile, columns), bf16),
            pltpu.VMEM((rows, columns), f32),
            pltpu.VMEM((rows, columns - lead), f32),
            pltpu.VMEM((rows, columns - lead), bf16),
            pltpu.VMEM((rows, columns - lead), bf16),
            dma((1 + width // tile,)),
            dma((2, chips)), dma((2, chips)),
            dma((2, chips)), dma((2, chips)),
            dma((1,)), dma((1,)),
            dma((n, slots, CHUNKS)), dma((n, slots, CHUNKS)), dma((n, slots, CHUNKS)),
            dma((2,)),
        ],
        compiler_params=pltpu.CompilerParams(
            collective_id=0, has_side_effects=True, vmem_limit_bytes=56 << 20
        ),
        cost_estimate=pl.CostEstimate(
            flops=2 * rows * n * slots * tile * columns,
            bytes_accessed=4 * rows * columns, transcendentals=0,
        ),
    )(tile_ids, amplitudes, integrals)


def solution(mesh):
    placed = (
        P(("groups", "fetch"), "blk"),
        P(("groups", "blk"), "fetch", None, None),
        P(("groups", "blk"), None),
    )
    return jax.shard_map(
        functools.partial(per_device, dict(mesh.shape)),
        mesh=mesh,
        in_specs=placed,
        out_specs=P(("groups", "fetch"), "blk"),
        check_vma=False,
    )
```

time: 156 us -> 89.6 us (0.57)
  waiting for transfers between devices: 115 us -> 0 us
  Pallas kernels: 0 us -> 87.3 us
  matrix products: 15.3 us -> 0 us
  between operations: 13.4 us -> 0.01 us
  starting transfers between devices: 5.11 us -> 0 us
  local copies, waits for them, and re-layouts: 6.18 us -> 2.16 us
    all_gather x1 -> x0, waiting for transfers between devices: 101 us -> none  [per_device(): gathered = lax.all_gather(integrals, 'fetch', axis=1, tiled=True)]
    pallas_call x0 -> x1, Pallas kernels: none -> 87.3 us  [per_device(): pl.pallas_call(functools.partial(kernel, n, chips, lead), out_shape=jax.S...]
    dot_general x5 -> x0, matrix products: 15.3 us -> none  [the longest x1 7.78 us: per_device(): jnp.einsum('ks,stc->ktc', selector, stacked, preferred_element_type=jnp.f...]
    ppermute x3 -> x0, waiting for transfers between devices: 13.5 us -> none  [from_behind(): return lax.ppermute(value, axis, pairs)]
    convert_element_type x1 -> x0, local copies, waits for them, and re-layouts: 6.17 us -> none  [per_device(): dense = dense.astype(jnp.bfloat16).reshape(tile_count * tile_width, columns)]
    ppermute x3 -> x0, starting transfers between devices: 5.11 us -> none  [from_behind(): return lax.ppermute(value, axis, pairs)]
    unnamed x4 -> x1, local copies, waits for them, and re-layouts: 0.01 us -> 2.16 us
  transfers between devices with their start and end apart: 4 -> 0, of which waited for: 2 -> 0; matrix products, arithmetic and copies ran while one was open for 13% -> 0% of each run, Pallas kernels for 0% -> 0%
where the time goes in v1:
time: 89.6 us; the launch traced here: 89.4 us
  Pallas kernels  87.3 us (97%)
  local copies, waits for them, and re-layouts  2.16 us (2%)
    pallas_call x1, Pallas kernels, per_device(): pl.pallas_call(functools.partial(kernel, n, chips, lead), out_shape=jax.S...  87.3 us
    unnamed x1, local copies, waits for them, and re-layouts  2.16 us

profile of v1, /device:TPU:0, one launch (start us, length us, event | category | flops | bytes accessed | tf_op | source)
XLA Modules:
  0.0 89.4 jit_solution(14528550461486055222)
XLA Ops:
  0.0 87.3 %shard_map.37 = bf16[448,1024]{1,0:T(8,128)(2,1)} custom-call(s32[1,12]{1,0:T(1,128)} %ids_ref.1, bf16[448,768]{1,0:T(8,128)(2,1)} %a_ref.1, bf16[1,3,256,1024]{3,2,1,0:T(8,128)(2,1)} %b_ref.1), custom_call_target="tpu_custom_call" | custom-call | flops 2818572288 | bytes 1835008 | tf_op jit(solution)/shard_map/pallas_call | solution.py:287
  87.3 2.2 %copy.5 = bf16[448,1024]{1,0:T(8,128)(2,1)} copy(bf16[448,1024]{1,0:T(8,128)(2,1)} %shard_map.37) | data formatting | bytes 1835008

commit v2 on v1

v2 whole, which is shorter than its diff:
```python
import functools

import jax
import jax.numpy as jnp
from jax import lax
from jax.experimental import pallas as pl
from jax.experimental.pallas import tpu as pltpu
from jax.sharding import PartitionSpec as P

CORES = 2
LAG = 4
MESH = pl.DeviceIdType.MESH


def kernel(
    n, chips, cuts,
    ids_ref, a_ref, b_ref, out_ref,
    abuf, aout, bbuf, acc, acc_first, acc_last, o_first, o_last, r_first, r_last,
    local_sem, a_send, a_recv, s_send, s_recv, o_send, o_recv,
    p_send, m_send, b_recv, r_send, r_recv,
):
    g = lax.axis_index("groups")
    b = lax.axis_index("blk")
    f = lax.axis_index("fetch")
    x, core = lax.div(b, CORES), lax.rem(b, CORES)
    sibling = b + 1 - 2 * core
    slots, tile, columns = b_ref.shape[1:]
    per_group = a_ref.shape[1] // tile
    spans = [slice(0, cuts[0]), slice(cuts[0], cuts[1]), slice(cuts[1], columns)]

    low = f < n // 2
    way = jnp.where(low, 1, -1)
    far_hops = jnp.where(low, n - 1 - f, f)
    near_hops = n - 1 - far_hops
    is_end = near_hops == 0
    is_helper = near_hops == 1
    has_near = near_hops > 0
    far_side = (g, b, jnp.clip(f + way, 0, n - 1))
    near_side = (g, b, jnp.clip(f - way, 0, n - 1))

    def mate(hop):
        return lax.rem(x + hop, chips) * CORES + core

    barrier = pltpu.get_barrier_semaphore()
    for hop in range(1, chips):
        pl.semaphore_signal(barrier, inc=1, device_id=(g, mate(hop), f), device_id_type=MESH)
    pl.semaphore_signal(barrier, inc=1, device_id=(g, sibling, f), device_id_type=MESH)
    pl.semaphore_signal(barrier, inc=1, device_id=far_side, device_id_type=MESH)

    @pl.when(has_near)
    def _():
        pl.semaphore_signal(barrier, inc=1, device_id=near_side, device_id_type=MESH)

    own_a = [
        pltpu.make_async_copy(
            a_ref.at[:, pl.ds(k * tile, tile)], abuf.at[b * per_group + k], local_sem.at[1 + k]
        )
        for k in range(per_group)
    ]
    own_b = pltpu.make_async_copy(b_ref.at[0], bbuf.at[f], local_sem.at[0])
    for copy in own_a:
        copy.start()
    own_b.start()
    for copy in own_a:
        copy.wait()
    pl.semaphore_wait(barrier, chips + 1 + jnp.where(has_near, 1, 0))

    def remote(src, dst, send, recv, device):
        return pltpu.make_async_remote_copy(
            src_ref=src, dst_ref=dst, send_sem=send, recv_sem=recv,
            device_id=device, device_id_type=MESH,
        )

    def b_copy(span, owner, slot, device, send, src=None):
        lanes = pl.ds(spans[span].start, spans[span].stop - spans[span].start)
        piece = bbuf.at[owner, slot, :, lanes]
        source = piece if src is None else src.at[0, slot, :, lanes]
        return remote(source, piece, send.at[owner, slot, span], b_recv.at[owner, slot, span], device)

    def to_far(span, owner, slot, src=None):
        return b_copy(span, owner, slot, far_side, p_send, src)

    def to_near(span, owner, slot, src=None):
        return b_copy(span, owner, slot, near_side, m_send, src)

    def sends_near(span):
        return has_near if span == 1 else near_hops > 1

    def a_group(buffer, owner):
        return buffer.at[pl.ds(owner * per_group, per_group)]

    def a_mate(buffer, hop, base):
        part = a_group(buffer, b)
        return remote(part, part, a_send.at[base, hop], a_recv.at[base, hop], (g, mate(hop), f))

    def a_sib(buffer, hop, base):
        part = a_group(buffer, lax.rem(x + chips - hop, chips) * CORES + core)
        return remote(part, part, s_send.at[base, hop], s_recv.at[base, hop], (g, sibling, f))

    def start_own(span):
        for slot in range(slots):
            to_far(span, f, slot, b_ref).start()

        @pl.when(sends_near(span))
        def _():
            for slot in range(slots):
                to_near(span, f, slot, b_ref).start()

    a_help = remote(a_group(abuf, b), a_group(aout, b), o_send.at[0], o_recv.at[0], far_side)

    @pl.when(is_end)
    def _():
        a_help.start()

    start_own(0)
    for hop in range(1, chips):
        a_mate(abuf, hop, 0).start()
    a_sib(abuf, 0, 0).start()

    @pl.when(jnp.logical_not(is_end))
    def _():
        start_own(1)

    acc[...] = jnp.zeros_like(acc)
    acc_first[...] = jnp.zeros_like(acc_first)
    acc_last[...] = jnp.zeros_like(acc_last)
    own_b.wait()

    def a_tile(buffer, owner, slot):
        name = ids_ref[0, owner * slots + slot]
        empty = lax.shift_right_arithmetic(name, 31)
        value = buffer[name - empty]
        return value * (1 + empty).astype(jnp.float32).astype(value.dtype)

    def add(span, owner, slot):
        part = spans[span]
        acc[:, part] += jnp.dot(
            a_tile(abuf, owner, slot), bbuf[owner, slot, :, part], preferred_element_type=jnp.float32
        )

    def add_help(span, total, owner, slot):
        total[...] += jnp.dot(
            a_tile(aout, owner, slot), bbuf[owner, slot, :, spans[span]],
            preferred_element_type=jnp.float32,
        )

    def item(index, hops, direction):
        tail = index - 2 * slots * hops
        late = tail >= 0
        span = jnp.where(late, 2, lax.rem(lax.div(index, slots), 2))
        distance = 1 + jnp.where(late, lax.div(tail, slots), lax.div(index, 2 * slots))
        return span, f + direction * distance, lax.rem(index, slots)

    def by_span(span, action):
        for which in range(3):
            @pl.when(span == which)
            def _(which=which):
                action(which)

    def far_item(index):
        return item(index, far_hops, way)

    def far_add(index):
        span, owner, slot = far_item(index)

        def one(which):
            if which == 1:
                add(which, owner, slot)
            else:
                pl.when(jnp.logical_not(is_end))(lambda: add(which, owner, slot))

        by_span(span, one)

    first_result = remote(o_first, r_first, r_send.at[0], r_recv.at[0], near_side)
    last_result = remote(o_last, r_last, r_send.at[1], r_recv.at[1], near_side)
    far_items = 3 * slots * far_hops
    near_items = 3 * slots * near_hops
    far_end = f + way * far_hops

    def step(j, carry):
        @pl.when(j == 3)
        def _():
            for hop in range(1, chips):
                a_mate(abuf, hop, 0).wait_recv()
                a_sib(abuf, hop, 0).start()

            @pl.when(is_end)
            def _():
                a_help.wait_send()
                start_own(1)

            @pl.when(is_helper)
            def _():
                a_help.wait_recv()
                for hop in range(1, chips):
                    a_mate(aout, hop, 1).start()
                a_sib(aout, 0, 1).start()

        @pl.when(is_helper & (j == 6))
        def _():
            for hop in range(1, chips):
                a_mate(aout, hop, 1).wait_recv()
                a_sib(aout, hop, 1).start()

        @pl.when(is_helper & (j == 7))
        def _():
            for hop in range(chips):
                a_sib(aout, hop, 1).wait_recv()

        @pl.when(is_helper & (j == far_items - 1))
        def _():
            def one(index, carry):
                owner, slot = lax.div(index, slots), lax.rem(index, slots)

                @pl.when(jnp.logical_not((owner == far_end) & (slot == slots - 1)))
                def _():
                    add_help(2, acc_last, owner, slot)
                return carry

            lax.fori_loop(0, n * slots, one, 0)

        span, owner, slot = far_item(j)

        def arrive(which):
            @pl.when(jnp.logical_not(is_end) if which != 1 else j >= 0)
            def _():
                to_near(which, owner, slot).wait_recv()

            @pl.when(sends_near(which))
            def _():
                to_near(which, owner, slot).start()

        by_span(span, arrive)

        @pl.when(is_helper & (j == far_items - 1))
        def _():
            add_help(2, acc_last, owner, slot)
            o_last[...] = acc_last[...].astype(o_last.dtype)
            last_result.start()

        back = j - LAG
        near = (back >= 0) & (back < near_items)
        near_span, near_owner, near_slot = item(jnp.maximum(back, 0), near_hops, -way)

        @pl.when(near)
        def _():
            def pass_on(which):
                to_far(which, near_owner, near_slot).wait_recv()
                to_far(which, near_owner, near_slot).start()

            by_span(near_span, pass_on)

        @pl.when(back == jnp.maximum(2 * slots * near_hops - 1, 0))
        def _():
            start_own(2)

        @pl.when(j == 4)
        def _():
            for hop in range(chips):
                a_sib(abuf, hop, 0).wait_recv()

            def own_slot(slot, carry):
                for which in range(3):
                    add(which, f, slot)
                return carry

            lax.fori_loop(0, slots, own_slot, 0)

            def early(index, carry):
                far_add(index)
                return carry

            lax.fori_loop(0, 4, early, 0)

        @pl.when(j >= 4)
        def _():
            far_add(j)

        @pl.when(near)
        def _():
            by_span(near_span, lambda which: add(which, near_owner, near_slot))

        @pl.when(is_helper & (j == 2 * slots * (far_hops - 1) + slots - 1))
        def _():
            def one(index, carry):
                add_help(0, acc_first, lax.div(index, slots), lax.rem(index, slots))
                return carry

            lax.fori_loop(0, n * slots, one, 0)
            o_first[...] = acc_first[...].astype(o_first.dtype)
            first_result.start()

        return carry

    lax.fori_loop(0, far_items, step, 0)

    out_ref[:, spans[1]] = acc[:, spans[1]].astype(out_ref.dtype)

    @pl.when(is_end)
    def _():
        first_result.wait_recv()
        out_ref[:, spans[0]] = r_first[...]
        last_result.wait_recv()
        out_ref[:, spans[2]] = r_last[...]

    @pl.when(jnp.logical_not(is_end))
    def _():
        for part in (spans[0], spans[2]):
            out_ref[:, part] = acc[:, part].astype(out_ref.dtype)

    def far_done(k, carry):
        owner, slot = f - way * lax.div(k, slots), lax.rem(k, slots)
        for which in range(3):
            to_far(which, owner, slot).wait_send()
        return carry

    lax.fori_loop(0, slots * (near_hops + 1), far_done, 0)

    def near_done(k, carry):
        owner, slot = f + way * lax.div(k, slots), lax.rem(k, slots)
        for which in range(3):
            @pl.when(sends_near(which))
            def _(which=which):
                to_near(which, owner, slot).wait_send()
        return carry

    lax.fori_loop(0, slots * (far_hops + 1), near_done, 0)

    for hop in range(1, chips):
        a_mate(abuf, hop, 0).wait_send()
    for hop in range(chips):
        a_sib(abuf, hop, 0).wait_send()

    @pl.when(is_helper)
    def _():
        for hop in range(1, chips):
            a_mate(aout, hop, 1).wait_send()
        for hop in range(chips):
            a_sib(aout, hop, 1).wait_send()
        first_result.wait_send()
        last_result.wait_send()


def per_device(mesh_shape, amplitudes, integrals, tile_ids):
    n, chips = mesh_shape["fetch"], mesh_shape["blk"] // CORES
    rows, width = amplitudes.shape
    _, slots, tile, columns = integrals.shape
    cuts = (columns * 3 // 8, columns * 7 // 8)
    first, last = cuts[0], columns - cuts[1]
    tiles = chips * CORES * width // tile
    bf16, f32, dma = jnp.bfloat16, jnp.float32, pltpu.SemaphoreType.DMA
    return pl.pallas_call(
        functools.partial(kernel, n, chips, cuts),
        out_shape=jax.ShapeDtypeStruct((rows, columns), bf16),
        in_specs=[
            pl.BlockSpec(memory_space=pltpu.SMEM),
            pl.BlockSpec(memory_space=pl.ANY),
            pl.BlockSpec(memory_space=pl.ANY),
        ],
        out_specs=pl.BlockSpec(memory_space=pltpu.VMEM),
        scratch_shapes=[
            pltpu.VMEM((tiles, rows, tile), bf16),
            pltpu.VMEM((tiles, rows, tile), bf16),
            pltpu.VMEM((n, slots, tile, columns), bf16),
            pltpu.VMEM((rows, columns), f32),
            pltpu.VMEM((rows, first), f32), pltpu.VMEM((rows, last), f32),
            pltpu.VMEM((rows, first), bf16), pltpu.VMEM((rows, last), bf16),
            pltpu.VMEM((rows, first), bf16), pltpu.VMEM((rows, last), bf16),
            dma((1 + width // tile,)),
            dma((2, chips)), dma((2, chips)),
            dma((2, chips)), dma((2, chips)),
            dma((1,)), dma((1,)),
            dma((n, slots, 3)), dma((n, slots, 3)), dma((n, slots, 3)),
            dma((2,)), dma((2,)),
        ],
        compiler_params=pltpu.CompilerParams(
            collective_id=0, has_side_effects=True, vmem_limit_bytes=56 << 20
        ),
        cost_estimate=pl.CostEstimate(
            flops=2 * rows * n * slots * tile * columns,
            bytes_accessed=4 * rows * columns, transcendentals=0,
        ),
    )(tile_ids, amplitudes, integrals)


def solution(mesh):
    placed = (
        P(("groups", "fetch"), "blk"),
        P(("groups", "blk"), "fetch", None, None),
        P(("groups", "blk"), None),
    )
    return jax.shard_map(
        functools.partial(per_device, dict(mesh.shape)),
        mesh=mesh,
        in_specs=placed,
        out_specs=P(("groups", "fetch"), "blk"),
        check_vma=False,
    )
```

time: 89.6 us -> 85.4 us (0.953)
  Pallas kernels: 87.3 us -> 83 us
    pallas_call x1, Pallas kernels: 87.3 us -> 83 us  [per_device(): pl.pallas_call(functools.partial(kernel, n, chips, cuts), out_shape=jax.S...]
where the time goes in v2:
time: 85.4 us; the launch traced here: 85.2 us
  Pallas kernels  83 us (97%)
  local copies, waits for them, and re-layouts  2.16 us (3%)
    pallas_call x1, Pallas kernels, per_device(): pl.pallas_call(functools.partial(kernel, n, chips, cuts), out_shape=jax.S...  83 us
    unnamed x1, local copies, waits for them, and re-layouts  2.16 us

profile of v2, /device:TPU:0, one launch (start us, length us, event | category | flops | bytes accessed | tf_op | source)
XLA Modules:
  0.0 85.2 jit_solution(18281674076480785954)
XLA Ops:
  0.0 83.0 %shard_map.37 = bf16[448,1024]{1,0:T(8,128)(2,1)} custom-call(s32[1,12]{1,0:T(1,128)} %ids_ref.1, bf16[448,768]{1,0:T(8,128)(2,1)} %a_ref.1, bf16[1,3,256,1024]{3,2,1,0:T(8,128)(2,1)} %b_ref.1), custom_call_target="tpu_custom_call" | custom-call | flops 2818572288 | bytes 1835008 | tf_op jit(solution)/shard_map/pallas_call | solution.py:352
  83.0 2.2 %copy.5 = bf16[448,1024]{1,0:T(8,128)(2,1)} copy(bf16[448,1024]{1,0:T(8,128)(2,1)} %shard_map.37) | data formatting | bytes 1835008

commit v3 on v2

--- a/solution.py
+++ b/solution.py
@@ -8,14 +8,14 @@
 from jax.sharding import PartitionSpec as P
 
 CORES = 2
-LAG = 4
+LAG = 3
 MESH = pl.DeviceIdType.MESH
 
 
 def kernel(
     n, chips, cuts,
     ids_ref, a_ref, b_ref, out_ref,
-    abuf, aout, bbuf, acc, acc_first, acc_last, o_first, o_last, r_first, r_last,
+    abuf, aout, bbuf, acc, total_0, total_2, total_3, o_0, o_2, o_3, r_0, r_2, r_3,
     local_sem, a_send, a_recv, s_send, s_recv, o_send, o_recv,
     p_send, m_send, b_recv, r_send, r_recv,
 ):
@@ -26,7 +26,8 @@
     sibling = b + 1 - 2 * core
     slots, tile, columns = b_ref.shape[1:]
     per_group = a_ref.shape[1] // tile
-    spans = [slice(0, cuts[0]), slice(cuts[0], cuts[1]), slice(cuts[1], columns)]
+    spans = [slice(cuts[k], cuts[k + 1]) for k in range(4)]
+    helped = {0: (total_0, o_0, r_0), 2: (total_2, o_2, r_2), 3: (total_3, o_3, r_3)}
 
     low = f < n // 2
     way = jnp.where(low, 1, -1)
@@ -112,7 +113,10 @@
     def _():
         a_help.start()
 
-    start_own(0)
+    @pl.when(jnp.logical_not(is_end))
+    def _():
+        start_own(0)
+
     for hop in range(1, chips):
         a_mate(abuf, hop, 0).start()
     a_sib(abuf, 0, 0).start()
@@ -122,8 +126,14 @@
         start_own(1)
 
     acc[...] = jnp.zeros_like(acc)
-    acc_first[...] = jnp.zeros_like(acc_first)
-    acc_last[...] = jnp.zeros_like(acc_last)
+    for total, _, _ in helped.values():
+        total[...] = jnp.zeros_like(total)
+
+    @pl.when(is_end)
+    def _():
+        a_help.wait_send()
+        start_own(0)
+
     own_b.wait()
 
     def a_tile(buffer, owner, slot):
@@ -138,7 +148,8 @@
             a_tile(abuf, owner, slot), bbuf[owner, slot, :, part], preferred_element_type=jnp.float32
         )
 
-    def add_help(span, total, owner, slot):
+    def add_help(span, owner, slot):
+        total = helped[span][0]
         total[...] += jnp.dot(
             a_tile(aout, owner, slot), bbuf[owner, slot, :, spans[span]],
             preferred_element_type=jnp.float32,
@@ -147,12 +158,14 @@
     def item(index, hops, direction):
         tail = index - 2 * slots * hops
         late = tail >= 0
-        span = jnp.where(late, 2, lax.rem(lax.div(index, slots), 2))
-        distance = 1 + jnp.where(late, lax.div(tail, slots), lax.div(index, 2 * slots))
+        third = tail >= slots * hops
+        within = jnp.where(third, tail - slots * hops, tail)
+        span = jnp.where(third, 3, jnp.where(late, 2, lax.rem(lax.div(index, slots), 2)))
+        distance = 1 + jnp.where(late, lax.div(within, slots), lax.div(index, 2 * slots))
         return span, f + direction * distance, lax.rem(index, slots)
 
     def by_span(span, action):
-        for which in range(3):
+        for which in range(4):
             @pl.when(span == which)
             def _(which=which):
                 action(which)
@@ -171,10 +184,18 @@
 
         by_span(span, one)
 
-    first_result = remote(o_first, r_first, r_send.at[0], r_recv.at[0], near_side)
-    last_result = remote(o_last, r_last, r_send.at[1], r_recv.at[1], near_side)
-    far_items = 3 * slots * far_hops
-    near_items = 3 * slots * near_hops
+    results = {
+        span: remote(out, landed, r_send.at[span], r_recv.at[span], near_side)
+        for span, (_, out, landed) in helped.items()
+    }
+
+    def give_back(span):
+        total, out, _ = helped[span]
+        out[...] = total[...].astype(out.dtype)
+        results[span].start()
+
+    far_items = 4 * slots * far_hops
+    near_items = 4 * slots * near_hops
     far_end = f + way * far_hops
 
     def step(j, carry):
@@ -183,11 +204,6 @@
             for hop in range(1, chips):
                 a_mate(abuf, hop, 0).wait_recv()
                 a_sib(abuf, hop, 0).start()
-
-            @pl.when(is_end)
-            def _():
-                a_help.wait_send()
-                start_own(1)
 
             @pl.when(is_helper)
             def _():
@@ -207,18 +223,6 @@
             for hop in range(chips):
                 a_sib(aout, hop, 1).wait_recv()
 
-        @pl.when(is_helper & (j == far_items - 1))
-        def _():
-            def one(index, carry):
-                owner, slot = lax.div(index, slots), lax.rem(index, slots)
-
-                @pl.when(jnp.logical_not((owner == far_end) & (slot == slots - 1)))
-                def _():
-                    add_help(2, acc_last, owner, slot)
-                return carry
-
-            lax.fori_loop(0, n * slots, one, 0)
-
         span, owner, slot = far_item(j)
 
         def arrive(which):
@@ -232,11 +236,11 @@
 
         by_span(span, arrive)
 
-        @pl.when(is_helper & (j == far_items - 1))
-        def _():
-            add_help(2, acc_last, owner, slot)
-            o_last[...] = acc_last[...].astype(o_last.dtype)
-            last_result.start()
+        for late in (2, 3):
+            @pl.when(is_helper & (span == late) & (owner == far_end))
+            def _(late=late):
+                add_help(late, owner, slot)
+                pl.when(slot == slots - 1)(lambda: give_back(late))
 
         back = j - LAG
         near = (back >= 0) & (back < near_items)
@@ -250,21 +254,21 @@
 
             by_span(near_span, pass_on)
 
-        @pl.when(back == jnp.maximum(2 * slots * near_hops - 1, 0))
-        def _():
-            start_own(2)
+        @pl.when(j == jnp.where(is_end, 4, -1))
+        def _():
+            for k in range(slots):
+                to_far(0, f, k).wait_send()
+            start_own(1)
+
+        for late in (2, 3):
+            @pl.when(j == jnp.where(is_end, 7 + late, late * slots * near_hops - 1 + LAG))
+            def _(late=late):
+                start_own(late)
 
         @pl.when(j == 4)
         def _():
             for hop in range(chips):
                 a_sib(abuf, hop, 0).wait_recv()
-
-            def own_slot(slot, carry):
-                for which in range(3):
-                    add(which, f, slot)
-                return carry
-
-            lax.fori_loop(0, slots, own_slot, 0)
 
             def early(index, carry):
                 far_add(index)
@@ -272,45 +276,66 @@
 
             lax.fori_loop(0, 4, early, 0)
 
+            @pl.when(has_near)
+            def _():
+                for passed in range(4 - LAG):
+                    add(0, f - way, passed)
+
         @pl.when(j >= 4)
         def _():
             far_add(j)
 
-        @pl.when(near)
+        @pl.when((j > 4) & (j <= 4 + slots))
+        def _():
+            for which in range(4):
+                add(which, f, j - 5)
+
+        @pl.when(near & (j >= 4))
         def _():
             by_span(near_span, lambda which: add(which, near_owner, near_slot))
 
+        def help_all(span, owners):
+            def one(index, carry):
+                add_help(span, lax.div(index, slots) + owners, lax.rem(index, slots))
+                return carry
+
+            return one
+
         @pl.when(is_helper & (j == 2 * slots * (far_hops - 1) + slots - 1))
         def _():
-            def one(index, carry):
-                add_help(0, acc_first, lax.div(index, slots), lax.rem(index, slots))
-                return carry
-
-            lax.fori_loop(0, n * slots, one, 0)
-            o_first[...] = acc_first[...].astype(o_first.dtype)
-            first_result.start()
+            lax.fori_loop(0, n * slots, help_all(0, 0), 0)
+            give_back(0)
+
+        for late in (2, 3):
+            @pl.when(is_helper & (j == slots * (late * far_hops + far_hops - 1) - 1))
+            def _(late=late):
+                skip = jnp.where(far_end == 0, 1, 0)
+                lax.fori_loop(0, (n - 1) * slots, help_all(late, skip), 0)
+
+        @pl.when(j == 2 * slots * far_hops)
+        def _():
+            for part in (spans[0], spans[1]):
+                out_ref[:, part] = acc[:, part].astype(out_ref.dtype)
 
         return carry
 
     lax.fori_loop(0, far_items, step, 0)
 
-    out_ref[:, spans[1]] = acc[:, spans[1]].astype(out_ref.dtype)
-
     @pl.when(is_end)
     def _():
-        first_result.wait_recv()
-        out_ref[:, spans[0]] = r_first[...]
-        last_result.wait_recv()
-        out_ref[:, spans[2]] = r_last[...]
+        for span, (_, _, landed) in helped.items():
+            results[span].wait_recv()
+            out_ref[:, spans[span]] = landed[...]
 
     @pl.when(jnp.logical_not(is_end))
     def _():
-        for part in (spans[0], spans[2]):
+        for part in (spans[2], spans[3]):
             out_ref[:, part] = acc[:, part].astype(out_ref.dtype)
 
     def far_done(k, carry):
         owner, slot = f - way * lax.div(k, slots), lax.rem(k, slots)
-        for which in range(3):
+        pl.when(jnp.logical_not(is_end))(lambda: to_far(0, owner, slot).wait_send())
+        for which in range(1, 4):
             to_far(which, owner, slot).wait_send()
         return carry
 
@@ -318,7 +343,7 @@
 
     def near_done(k, carry):
         owner, slot = f + way * lax.div(k, slots), lax.rem(k, slots)
-        for which in range(3):
+        for which in range(4):
             @pl.when(sends_near(which))
             def _(which=which):
                 to_near(which, owner, slot).wait_send()
@@ -337,16 +362,16 @@
             a_mate(aout, hop, 1).wait_send()
         for hop in range(chips):
             a_sib(aout, hop, 1).wait_send()
-        first_result.wait_send()
-        last_result.wait_send()
+        for result in results.values():
+            result.wait_send()
 
 
 def per_device(mesh_shape, amplitudes, integrals, tile_ids):
     n, chips = mesh_shape["fetch"], mesh_shape["blk"] // CORES
     rows, width = amplitudes.shape
     _, slots, tile, columns = integrals.shape
-    cuts = (columns * 3 // 8, columns * 7 // 8)
-    first, last = cuts[0], columns - cuts[1]
+    cuts = tuple(columns * eighths // 8 for eighths in (0, 2, 6, 7, 8))
+    helped = [cuts[k + 1] - cuts[k] for k in (0, 2, 3)]
     tiles = chips * CORES * width // tile
     bf16, f32, dma = jnp.bfloat16, jnp.float32, pltpu.SemaphoreType.DMA
     return pl.pallas_call(
@@ -363,15 +388,13 @@
             pltpu.VMEM((tiles, rows, tile), bf16),
             pltpu.VMEM((n, slots, tile, columns), bf16),
             pltpu.VMEM((rows, columns), f32),
-            pltpu.VMEM((rows, first), f32), pltpu.VMEM((rows, last), f32),
-            pltpu.VMEM((rows, first), bf16), pltpu.VMEM((rows, last), bf16),
-            pltpu.VMEM((rows, first), bf16), pltpu.VMEM((rows, last), bf16),
+            *[pltpu.VMEM((rows, size), kind) for kind in (f32, bf16, bf16) for size in helped],
             dma((1 + width // tile,)),
             dma((2, chips)), dma((2, chips)),
             dma((2, chips)), dma((2, chips)),
             dma((1,)), dma((1,)),
-            dma((n, slots, 3)), dma((n, slots, 3)), dma((n, slots, 3)),
-            dma((2,)), dma((2,)),
+            dma((n, slots, 4)), dma((n, slots, 4)), dma((n, slots, 4)),
+            dma((4,)), dma((4,)),
         ],
         compiler_params=pltpu.CompilerParams(
             collective_id=0, has_side_effects=True, vmem_limit_bytes=56 << 20

time: 85.4 us -> 83.7 us (0.980)
  Pallas kernels: 83 us -> 81.3 us
    pallas_call x1, Pallas kernels: 83 us -> 81.3 us  [per_device(): pl.pallas_call(functools.partial(kernel, n, chips, cuts), out_shape=jax.S...]
where the time goes in v3:
time: 83.7 us; the launch traced here: 83.5 us
  Pallas kernels  81.3 us (97%)
  local copies, waits for them, and re-layouts  2.16 us (3%)
    pallas_call x1, Pallas kernels, per_device(): pl.pallas_call(functools.partial(kernel, n, chips, cuts), out_shape=jax.S...  81.3 us
    unnamed x1, local copies, waits for them, and re-layouts  2.16 us

profile of v3, /device:TPU:0, one launch (start us, length us, event | category | flops | bytes accessed | tf_op | source)
XLA Modules:
  0.0 83.5 jit_solution(9495007323297917406)
XLA Ops:
  0.0 81.3 %shard_map.37 = bf16[448,1024]{1,0:T(8,128)(2,1)} custom-call(s32[1,12]{1,0:T(1,128)} %ids_ref.1, bf16[448,768]{1,0:T(8,128)(2,1)} %a_ref.1, bf16[1,3,256,1024]{3,2,1,0:T(8,128)(2,1)} %b_ref.1), custom_call_target="tpu_custom_call" | custom-call | flops 2818572288 | bytes 1835008 | tf_op jit(solution)/shard_map/pallas_call | solution.py:377
  81.3 2.2 %copy.5 = bf16[448,1024]{1,0:T(8,128)(2,1)} copy(bf16[448,1024]{1,0:T(8,128)(2,1)} %shard_map.37) | data formatting | bytes 1835008

commit v4 on v3

--- a/solution.py
+++ b/solution.py
@@ -261,7 +261,7 @@
             start_own(1)
 
         for late in (2, 3):
-            @pl.when(j == jnp.where(is_end, 7 + late, late * slots * near_hops - 1 + LAG))
+            @pl.when(j == jnp.where(is_end, 7 + late, late * slots * near_hops + LAG))
             def _(late=late):
                 start_own(late)
 

time: 83.7 us -> 85.1 us (1.017)
  Pallas kernels: 81.3 us -> 82.7 us
    pallas_call x1, Pallas kernels: 81.3 us -> 82.7 us  [per_device(): pl.pallas_call(functools.partial(kernel, n, chips, cuts), out_shape=jax.S...]
where the time goes in v4:
time: 85.1 us; the launch traced here: 84.9 us
  Pallas kernels  82.7 us (97%)
  local copies, waits for them, and re-layouts  2.16 us (3%)
    pallas_call x1, Pallas kernels, per_device(): pl.pallas_call(functools.partial(kernel, n, chips, cuts), out_shape=jax.S...  82.7 us
    unnamed x1, local copies, waits for them, and re-layouts  2.16 us

profile of v4, /device:TPU:0, one launch (start us, length us, event | category | flops | bytes accessed | tf_op | source)
XLA Modules:
  0.0 84.9 jit_solution(14224860148436526749)
XLA Ops:
  0.0 82.7 %shard_map.37 = bf16[448,1024]{1,0:T(8,128)(2,1)} custom-call(s32[1,12]{1,0:T(1,128)} %ids_ref.1, bf16[448,768]{1,0:T(8,128)(2,1)} %a_ref.1, bf16[1,3,256,1024]{3,2,1,0:T(8,128)(2,1)} %b_ref.1), custom_call_target="tpu_custom_call" | custom-call | flops 2818572288 | bytes 1835008 | tf_op jit(solution)/shard_map/pallas_call | solution.py:377
  82.8 2.2 %copy.5 = bf16[448,1024]{1,0:T(8,128)(2,1)} copy(bf16[448,1024]{1,0:T(8,128)(2,1)} %shard_map.37) | data formatting | bytes 1835008
